TPU v7x, 128 devices: a whole 4x4x4 slice. The times are simulated.
128 devices in a mesh: tile: 16 (over y, z), chan: 8 (over x, core).
Axes of the slice: x: 4, y: 4, z: 4, core: 2. Of those that a mesh axis runs over, the one named last changes fastest.
Arguments:
- grid: bfloat16 [512, 256, 256], P('chan', 'tile'), may hold values from -6 to 6
- station_feats: bfloat16 [512, 8192], P('chan', 'tile'), may hold values from -6 to 6
- owner_tile: int32 [8192, 1], P('tile'), may hold values from 0 to 15; in each aligned block of 512 rows (0 to 511, 512 to 1023, ...) at most 64 rows name the same one
- station_cell: int32 [8192], P('tile'), may hold values from 0 to 4095
- valid: int32 [8192], P('tile'), may hold values 0 or 1
- conv_first: bfloat16 [3, 3, 512, 512], P(None, None, None, 'chan'), may hold values from -0.09375 to 0.09375
- conv_second: bfloat16 [3, 3, 512, 512], P(None, None, None, 'chan'), may hold values from -0.09375 to 0.09375
- grad_out: bfloat16 [512, 256, 256], P('chan', 'tile'), may hold values from -6 to 6
Outputs:
- output: bfloat16 [512, 256, 256], P('chan', 'tile')
- grad_weight: bfloat16 [3, 3, 512, 512], P(None, None, 'tile', 'chan')
- grad_hidden: bfloat16 [512, 256, 256], P('chan', 'tile')
Inputs may be any that keep to these rules, and one draw needn't show every extreme that they name: `owner_tile`: among the 512 rows of one tile shard, at most 64 name one tile.
All inputs are finite; a program needn't handle non-finite values. No bound on the sum of `valid` on one device may be relied on, other than what follows from the above.
Results may differ from a plain program's by a relative error of at most 0.0051.
Values may be sent and summed in bfloat16 or wider, within the bound.
A program may use at most 128 MiB of HBM per device.

v0:
```python
import jax
import jax.numpy as jnp
from jax import lax
from jax.experimental import pallas as pl
from jax.experimental.pallas import tpu as pltpu
from jax.sharding import PartitionSpec as P

MESH = pl.DeviceIdType.MESH
BF16 = jnp.bfloat16
F32 = jnp.float32

CH = 64
ROWS = 16
COLS = 256
CELLS = ROWS * COLS
LANES = CELLS + 2 * COLS
BLOCK = CELLS // 2
TILES = 16
CHANS = 8
ALL = CH * CHANS
SHARD = 512
CAP = 64
PACK = 80
PART = 32
NT = (((1,), (1,)), ((), ()))

G, A, H = 0, 1, 2


def shifted(values, by):
    lanes = values.shape[1]
    col = lax.broadcasted_iota(jnp.int32, values.shape, 1) % COLS
    if by == 1:
        return jnp.where(col == 0, 0.0, pltpu.roll(values, 1, 1))
    return jnp.where(col == COLS - 1, 0.0, pltpu.roll(values, lanes - 1, 1))


def neighbour_sum(z):
    return z[CH : 2 * CH] + shifted(z[:CH], 1) + shifted(z[2 * CH :], -1)


def kernel(
    grid_ref, gout_ref, feats_ref, marks_ref, w1_ref, w2_ref,
    out_ref, gw_ref, gh_ref,
    ga, aa, ha, zbuf, hidden_pre, h3, b2, wb, wbt, packed, landed, masked,
    gw_out, gw_one, gw_mid, gw_two, gw_fin, gw_land,
    x_send, x_recv, e_send, e_recv, d_send, d_recv, s_send, s_recv, w_send, w_recv, v_send, v_recv,
    one_send, one_recv, two_send, two_recv, three_send, three_recv,
):
    tile = lax.axis_index("tile")
    chan = lax.axis_index("chan")
    x, core = chan // 2, chan % 2
    y, z = tile // 4, tile % 4
    bufs = (ga, aa, ha)
    chips = [x, (x + 3) % 4, (x + 1) % 4, (x + 2) % 4]
    right = (tile, chips[2] * 2 + core)
    left = (tile, chips[1] * 2 + core)
    sibling = (tile, x * 2 + (1 - core))
    has_up, has_down = tile > 0, tile < TILES - 1

    barrier = pltpu.get_barrier_semaphore()
    for step in range(1, TILES):
        pl.semaphore_signal(barrier, inc=1, device_id=((tile + step) % TILES, chan), device_id_type=MESH)
    for step in range(1, CHANS):
        pl.semaphore_signal(barrier, inc=1, device_id=(tile, (chan + step) % CHANS), device_id_type=MESH)

    def rows_of(chip, which, low=0, size=CH):
        return pl.ds(pl.multiple_of(chip * (2 * CH) + which * CH + low, size), size)

    def pair_of(chip):
        return pl.ds(pl.multiple_of(chip * (2 * CH), 2 * CH), 2 * CH)

    own = rows_of(x, core)
    halves = (pl.ds(COLS, BLOCK), pl.ds(COLS + BLOCK, BLOCK))
    quarters = [pl.ds(COLS + q * 1024, 1024) for q in range(4)]
    top, bottom = pl.ds(0, COLS), pl.ds(COLS + CELLS, COLS)
    first, last = pl.ds(COLS, COLS), pl.ds(CELLS, COLS)
    inner = pl.ds(COLS, CELLS)

    def remote(src, dst, send, recv, device):
        return pltpu.make_async_remote_copy(
            src_ref=src, dst_ref=dst, send_sem=send, recv_sem=recv, device_id=device, device_id_type=MESH
        )

    x_table = (
        (0, halves[0], 0, CH, True, 1),
        (0, halves[1], 0, CH, True, 1),
        (0, halves[0], 0, CH, False, 2),
        (0, halves[1], 0, CH, False, 2),
        (1, halves[0], 0, CH // 2, True, 3),
        (1, quarters[3], 0, CH // 2, True, 3),
        (1, quarters[2], 0, CH // 2, True, 3),
        (2, halves[0], CH // 2, CH // 2, False, 3),
        (2, quarters[3], CH // 2, CH // 2, False, 3),
        (2, quarters[2], CH // 2, CH // 2, False, 3),
    )

    def x_copy(f, k, arriving=False):
        sent, lanes, low, size, to_right, received = x_table[k]
        place = bufs[f].at[rows_of(chips[received if arriving else sent], core, low, size), lanes]
        return remote(place, place, x_send.at[f, k], x_recv.at[f, k], right if to_right else left)

    def e_copy(f, j, down, arriving=False):
        rows = rows_of(chips[j], core)
        k = 2 * j + down
        src = bufs[f].at[rows, last if down else first]
        dst = bufs[f].at[rows, top if down else bottom]
        device = (jnp.minimum(tile + 1, TILES - 1) if down else jnp.maximum(tile - 1, 0), chan)
        return remote(dst if arriving else src, dst, e_send.at[f, k], e_recv.at[f, k], device)

    def e_start(f, j, down):
        @pl.when(has_down if down else has_up)
        def _():
            e_copy(f, j, down).start()

    def e_wait_recv(f, j, down):
        @pl.when(has_up if down else has_down)
        def _():
            e_copy(f, j, down, True).wait_recv()

    d_table = (
        (0, pl.ds(0, LANES)),
        (1, pl.ds(0, LANES)),
        (2, pl.ds(0, LANES)),
        (3, halves[0]),
        (3, quarters[3]),
        (3, quarters[2]),
        (3, top),
        (3, bottom),
    )

    def d_copy(f, k, arriving=False):
        j, lanes = d_table[k]
        place = bufs[f].at[rows_of(chips[j], 1 - core if arriving else core), lanes]
        return remote(place, place, d_send.at[f, k], d_recv.at[f, k], sibling)

    def own_start(f, half):
        x_copy(f, half).start()
        x_copy(f, 2 + half).start()
        e_start(f, 0, half)

    def pass_on(f, j):
        e_wait_recv(f, j, 1)
        e_wait_recv(f, j, 0)
        d_copy(f, j).start()

    def forward(f, ks):
        for k in ks:
            x_copy(f, k).start()

    def near(f, onward):
        x_copy(f, 0, True).wait_recv()
        if onward:
            forward(f, (4,))
        e_start(f, 1, 0)
        x_copy(f, 2, True).wait_recv()
        if onward:
            forward(f, (7,))
        e_start(f, 2, 0)
        x_copy(f, 1, True).wait_recv()
        if onward:
            forward(f, (5, 6))
        e_start(f, 1, 1)
        x_copy(f, 3, True).wait_recv()
        if onward:
            forward(f, (8, 9))
        e_start(f, 2, 1)

    def far(f):
        x_copy(f, 4, True).wait_recv()
        x_copy(f, 7, True).wait_recv()
        e_start(f, 3, 0)
        d_copy(f, 3).start()
        x_copy(f, 5, True).wait_recv()
        x_copy(f, 8, True).wait_recv()
        e_start(f, 3, 1)
        d_copy(f, 4).start()
        x_copy(f, 6, True).wait_recv()
        x_copy(f, 9, True).wait_recv()
        d_copy(f, 5).start()

    def far_edges(f):
        e_wait_recv(f, 3, 1)
        d_copy(f, 6).start()
        e_wait_recv(f, 3, 0)
        d_copy(f, 7).start()

    def d_wait(f, j):
        for k in range(len(d_table)):
            if d_table[k][0] == j:
                d_copy(f, k, True).wait_recv()

    def products(buf, weights, pairs, block):
        total = None
        for r in range(3):
            lanes = pl.ds(pl.multiple_of(block * BLOCK + r * COLS, COLS), BLOCK)
            taps = pl.ds(r * 3 * CH, 3 * CH)
            if pairs is None:
                lhs, rhs = weights[taps, :], buf[:, lanes]
            else:
                lhs = [weights[taps, pair_of(p)] for p in pairs]
                rhs = [buf[pair_of(p), lanes] for p in pairs]
                lhs = lhs[0] if len(lhs) == 1 else jnp.concatenate(lhs, axis=1)
                rhs = rhs[0] if len(rhs) == 1 else jnp.concatenate(rhs, axis=0)
            term = jnp.dot(lhs, rhs, preferred_element_type=F32)
            total = term if total is None else total + term
        return total

    def conv_pass(buf, weights, pairs, start):
        @pl.loop(0, 2)
        def _(block):
            terms = products(buf, weights, pairs, block)
            zbuf[block] = terms if start else zbuf[block] + terms

    def block_lanes(block, skip=0):
        return pl.ds(pl.multiple_of(block * BLOCK + skip, COLS), BLOCK)

    def block_rows(block):
        return pl.ds(pl.multiple_of(block * (ROWS // 2), ROWS // 2), ROWS // 2)

    with jax.named_scope("prepare"):
        ga[own, inner] = gout_ref[...].reshape(CH, CELLS)
        for buf in bufs:
            for chip in chips:
                @pl.when(tile == 0)
                def _(buf=buf, chip=chip):
                    buf[rows_of(chip, core), top] = jnp.zeros((CH, COLS), BF16)

                @pl.when(tile == TILES - 1)
                def _(buf=buf, chip=chip):
                    buf[rows_of(chip, core), bottom] = jnp.zeros((CH, COLS), BF16)

        marks = marks_ref[...]
        columns = marks.astype(F32).T
        owners, usable = columns[:, 0:1].astype(jnp.int32), columns[:, 1:2] == 1.0
        tile_of = lax.broadcasted_iota(jnp.int32, (SHARD, 128), 1)
        named = jnp.where((owners == tile_of) & usable, 1.0, 0.0)
        lower = lax.broadcasted_iota(jnp.int32, (SHARD, SHARD), 0) >= lax.broadcasted_iota(jnp.int32, (SHARD, SHARD), 1)
        counts = jnp.dot(jnp.where(lower, 1.0, 0.0).astype(BF16), named.astype(BF16), preferred_element_type=F32)
        rank = jnp.sum(counts * named, axis=1, keepdims=True).astype(jnp.int32) - 1
        slot = jnp.where(usable, owners * 128 + (tile % 2) * CAP + rank, -1)
        cells = marks[2:3]
        sub = lax.broadcasted_iota(jnp.int32, (PACK - CH, SHARD), 0)
        places = jnp.where(sub == 0, cells // COLS, jnp.where(sub == 1, cells % COLS, 0))
        rowed = jnp.concatenate([feats_ref[...], places.astype(F32).astype(BF16)], axis=0)
        for part in range(4):
            number = lax.broadcasted_iota(jnp.int32, (SHARD, 512), 1) + part * 512
            chosen = jnp.where(slot == number, 1.0, 0.0).astype(BF16)
            sent = jnp.dot(rowed, chosen, preferred_element_type=F32).astype(BF16)
            for k in range(4):
                packed[part * 4 + k] = sent[:, k * 128 : (k + 1) * 128]
        landed[tile] = packed[tile]

    with jax.named_scope("barrier_wait"):
        pl.semaphore_wait(barrier, TILES + CHANS - 2)

    def s_copy(step, arriving=False):
        other = (tile + step) % TILES
        place = landed.at[(tile + TILES - step) % TILES]
        if arriving:
            return remote(place, place, s_send.at[step], s_recv.at[step], (other, chan))
        return remote(packed.at[other], landed.at[tile], s_send.at[step], s_recv.at[step], (other, chan))

    def w_copy(step, arriving=False):
        other = (chan + step) % CHANS
        rows = pl.ds(pl.multiple_of(z * 16, 16), 16)
        place = wb.at[(chan + CHANS - step) % CHANS, rows]
        if arriving:
            return remote(place, place, w_send.at[step], w_recv.at[step], (tile, other))
        return remote(b2.at[other, rows], wb.at[chan, rows], w_send.at[step], w_recv.at[step], (tile, other))

    def v_copy(step, arriving=False):
        other = y * 4 + (z + step) % 4
        quarter = (z + 4 - step) % 4 if arriving else z
        place = wb.at[:, pl.ds(pl.multiple_of(quarter * 16, 16), 16)]
        return remote(place, place, v_send.at[step], v_recv.at[step], (other, chan))

    with jax.named_scope("first_sends"):
        for step in range(1, TILES):
            s_copy(step).start()
        own_start(G, 0)
        own_start(G, 1)

    with jax.named_scope("weight_pieces"):
        lane = lax.broadcasted_iota(jnp.int32, (CH, 128), 1)
        for chip in range(4):
            taps = [w2_ref[pl.ds((8 - n) * CH, CH), pl.ds(chip * 128, 128)].astype(F32) for n in range(9)]
            turned = [pltpu.roll(tap, CH, 1) for tap in taps]
            for k in range(5):
                n = 2 * k
                even = jnp.where(lane < CH, taps[n], turned[n + 1] if n < 8 else 0.0)
                odd = jnp.where(lane < CH, turned[n], taps[n + 1] if n < 8 else 0.0)
                b2[2 * chip, :, pl.ds(k * 128, 128)] = even.astype(BF16)
                b2[2 * chip + 1, :, pl.ds(k * 128, 128)] = odd.astype(BF16)
        for step in range(1, CHANS):
            w_copy(step).start()
        mine = pl.ds(pl.multiple_of(z * 16, 16), 16)
        wb[chan, mine] = b2[chan, mine]

    with jax.named_scope("station_wait"):
        for step in range(1, TILES):
            s_copy(step, True).wait_recv()
    with jax.named_scope("assimilate"):
        stations = jnp.concatenate([landed[2 * k] + landed[2 * k + 1] for k in range(TILES // 2)], axis=1)
        slots = stations.shape[1]
        station_row = stations[CH : CH + 1].astype(F32)
        station_col = stations[CH + 1 : CH + 2].astype(F32)
        spread = lax.broadcasted_iota(jnp.int32, (COLS, slots), 0).astype(F32)
        col_hot = jnp.where(station_col == spread, 1.0, 0.0).astype(BF16)
        features = stations[:CH].astype(F32)
        for i in range(ROWS):
            masked[pl.ds(i * CH, CH), :] = jnp.where(station_row == float(i), features, 0.0).astype(BF16)
        background = grid_ref[...].reshape(CH, CELLS)
        for half in range(2):
            rows = pl.ds(half * 512, 512)
            sums = lax.dot_general(masked[rows, :], col_hot, NT, preferred_element_type=F32)
            for k in range(8):
                i = half * 8 + k
                value = background[:, i * COLS : (i + 1) * COLS].astype(F32) + sums[k * CH : (k + 1) * CH]
                aa[own, pl.ds((i + 1) * COLS, COLS)] = value.astype(BF16)
            own_start(A, half)

    with jax.named_scope("pass_on_0"):
        pass_on(G, 0)
        for step in range(1, CHANS):
            w_copy(step, True).wait_recv()
        for step in range(1, 4):
            v_copy(step).start()
        pass_on(A, 0)
    with jax.named_scope("wait_A0"):
        d_wait(A, 0)
    with jax.named_scope("conv1_pass1"):
        conv_pass(aa, w1_ref, [chips[0]], True)
    with jax.named_scope("near_G"):
        near(G, False)
        pass_on(G, 1)
        pass_on(G, 2)
    with jax.named_scope("turn_weights"):
        for step in range(1, 4):
            v_copy(step, True).wait_recv()
        for s in range(CHANS // 2):
            two = jnp.concatenate([wb[2 * s], wb[2 * s + 1]], axis=0).astype(F32)
            wbt[:, pl.ds(s * 128, 128)] = two.T.astype(BF16)
    with jax.named_scope("near_A"):
        near(A, True)
        pass_on(A, 1)
        pass_on(A, 2)
    with jax.named_scope("wait_A12"):
        d_wait(A, 1)
        d_wait(A, 2)
    with jax.named_scope("conv1_pass2"):
        conv_pass(aa, w1_ref, [chips[1], chips[2]], False)
    with jax.named_scope("far_A"):
        far(A)
        forward(G, (4, 7, 5, 8, 6, 9))
        far_edges(A)
    with jax.named_scope("wait_A3"):
        d_wait(A, 3)
    with jax.named_scope("conv1_pass3"):
        for half in range(2):
            value = neighbour_sum(zbuf[half] + products(aa, w1_ref, [chips[3]], half))
            hidden_pre[:, block_lanes(half)] = value
            hidden = value * (1.0 / (1.0 + jnp.exp(-value)))
            ha[own, block_lanes(half, COLS)] = hidden.astype(BF16)
            own_start(H, half)

    def weight_terms(group):
        for r in range(3):
            lanes = pl.ds((2 - r) * COLS, CELLS)
            against = jnp.concatenate([ga[pair_of(chips[2 * group + k]), lanes] for k in range(2)], axis=0)
            term = lax.dot_general(h3[...], against, NT, preferred_element_type=F32).astype(BF16)
            for part in range(2):
                gw_out[part, r, :, pl.ds(group * 256, 256)] = term[part * 96 : (part + 1) * 96]

    group_lanes = (pl.ds(0, 256), pl.ds(256, 256))
    collects = z // 2 == core
    owns = collects & (y == x)

    def one_copy(part, group):
        target = 2 * core + part
        slot = jnp.maximum((target + 4 - z) % 4 - 1, 0)
        return remote(
            gw_out.at[part, :, :, group_lanes[group]],
            gw_one.at[slot, :, :, group_lanes[group]],
            one_send.at[part, group],
            one_recv.at[slot, group],
            (y * 4 + target, chan),
        )

    def one_start(group):
        for part in range(2):
            @pl.when(2 * core + part != z)
            def _(part=part):
                one_copy(part, group).start()

    def two_copy(group):
        slot = jnp.maximum((x + 4 - y) % 4 - 1, 0)
        return remote(
            gw_mid.at[:, :, group_lanes[group]],
            gw_two.at[slot, :, :, group_lanes[group]],
            two_send.at[group],
            two_recv.at[slot, group],
            (x * 4 + z, chan),
        )

    def slot_wait(buf, recv, slot, group):
        place = buf.at[slot, :, :, group_lanes[group]]
        remote(place, place, recv.at[slot, group], recv.at[slot, group], (tile, chan)).wait_recv()

    def collect(group):
        @pl.when(collects)
        def _():
            for slot in range(3):
                slot_wait(gw_one, one_recv, slot, group)
            lanes = group_lanes[group]
            total = gw_out[z % 2, :, :, lanes].astype(F32)
            for slot in range(3):
                total = total + gw_one[slot, :, :, lanes].astype(F32)
            gw_mid[:, :, lanes] = total.astype(BF16)

            @pl.when(y != x)
            def _():
                two_copy(group).start()

    def finish(group):
        @pl.when(owns)
        def _():
            for slot in range(3):
                slot_wait(gw_two, two_recv, slot, group)
            lanes = group_lanes[group]
            total = gw_mid[:, :, lanes].astype(F32)
            for slot in range(3):
                total = total + gw_two[slot, :, :, lanes].astype(F32)
            gw_fin[:, :, lanes] = total.astype(BF16)
            for k in range(2):
                j = 2 * group + k
                for which in range(2):
                    if j == 0:
                        @pl.when(core != which)
                        def _(j=j, which=which):
                            three_copy(j, which).start()
                    else:
                        three_copy(j, which).start()
            if group == 0:
                gw_land[...] = gw_fin[:, :, pl.ds(0, 128)]

    def three_copy(j, which):
        return remote(
            gw_fin.at[:, :, pl.ds(j * 128, 128)],
            gw_land,
            three_send.at[j, which],
            three_recv.at[0],
            (tile, chips[j] * 2 + which),
        )

    with jax.named_scope("hidden_columns"):
        mine_h = ha[own, inner].astype(F32)
        moved = (shifted(mine_h, 1), mine_h, shifted(mine_h, -1))
        for part in range(2):
            for q in range(3):
                h3[pl.ds(part * 96 + q * PART, PART), :] = moved[q][part * PART : (part + 1) * PART].astype(BF16)
    with jax.named_scope("weight_terms_0"):
        d_wait(G, 0)
        d_wait(G, 1)
        d_wait(G, 2)
        weight_terms(0)
        one_start(0)
    with jax.named_scope("pass_on_H0"):
        pass_on(H, 0)
    with jax.named_scope("far_G"):
        far(G)
        far_edges(G)
        d_wait(G, 3)
    with jax.named_scope("weight_terms_1"):
        weight_terms(1)
        one_start(1)
    with jax.named_scope("grad_hidden"):
        @pl.loop(0, 2)
        def _(block):
            grad_act = neighbour_sum(products(ga, wbt, None, block))
            value = hidden_pre[:, block_lanes(block)]
            s = 1.0 / (1.0 + jnp.exp(-value))
            result = (grad_act * s * (1.0 + value * (1.0 - s))).astype(BF16)
            gh_ref[:, block_rows(block), :] = result.reshape(CH, ROWS // 2, COLS)
    with jax.named_scope("near_H"):
        near(H, True)
        pass_on(H, 1)
        pass_on(H, 2)
    with jax.named_scope("collect_0"):
        collect(0)
    with jax.named_scope("conv2_pass1"):
        d_wait(H, 0)
        conv_pass(ha, w2_ref, [chips[0]], True)
    with jax.named_scope("collect_1"):
        collect(1)
    with jax.named_scope("conv2_pass2"):
        d_wait(H, 1)
        d_wait(H, 2)
        conv_pass(ha, w2_ref, [chips[1], chips[2]], False)
    with jax.named_scope("far_H"):
        far(H)
        far_edges(H)
    with jax.named_scope("finish"):
        finish(0)
        finish(1)
    with jax.named_scope("wait_H3"):
        d_wait(H, 3)
    with jax.named_scope("conv2_pass3"):
        for half in range(2):
            branch = neighbour_sum(zbuf[half] + products(ha, w2_ref, [chips[3]], half))
            result = (aa[own, block_lanes(half, COLS)].astype(F32) + branch).astype(BF16)
            out_ref[:, half * (ROWS // 2) : (half + 1) * (ROWS // 2), :] = result.reshape(CH, ROWS // 2, COLS)
    with jax.named_scope("grad_weight"):
        @pl.when(jnp.logical_not(owns))
        def _():
            remote(gw_land, gw_land, three_recv.at[0], three_recv.at[0], (tile, chan)).wait_recv()

        for r in range(3):
            piece = gw_land[r].astype(F32)
            piece = jnp.where(core == 0, piece, pltpu.roll(piece, CH, 1))[:, :CH].astype(BF16)
            for q in range(3):
                gw_ref[r, q] = piece[q * PART : (q + 1) * PART]

    with jax.named_scope("sends_done"):
        for f in (G, A, H):
            for k in range(len(x_table)):
                x_copy(f, k).wait_send()
            for k in range(len(d_table)):
                d_copy(f, k).wait_send()
            for j in range(4):
                @pl.when(has_up)
                def _(f=f, j=j):
                    e_copy(f, j, 0).wait_send()

                @pl.when(has_down)
                def _(f=f, j=j):
                    e_copy(f, j, 1).wait_send()

        for step in range(1, TILES):
            s_copy(step).wait_send()
        for step in range(1, CHANS):
            w_copy(step).wait_send()
        for step in range(1, 4):
            v_copy(step).wait_send()
        for group in range(2):
            for part in range(2):
                @pl.when(2 * core + part != z)
                def _(part=part, group=group):
                    one_copy(part, group).wait_send()

            @pl.when(collects & (y != x))
            def _(group=group):
                two_copy(group).wait_send()

        @pl.when(owns)
        def _():
            for j in range(4):
                for which in range(2):
                    if j == 0:
                        @pl.when(core != which)
                        def _(j=j, which=which):
                            three_copy(j, which).wait_send()
                    else:
                        three_copy(j, which).wait_send()


def local(grid, station_feats, owner_tile, station_cell, valid, conv_first, conv_second, grad_out):
    w1 = conv_first.transpose(0, 1, 3, 2).reshape(9 * CH, ALL)
    w2 = conv_second.transpose(0, 1, 3, 2).reshape(9 * CH, ALL)
    marks = jnp.concatenate(
        [owner_tile.reshape(1, SHARD), valid.reshape(1, SHARD), station_cell.reshape(1, SHARD), jnp.zeros((5, SHARD), jnp.int32)]
    )
    vmem = pl.BlockSpec(memory_space=pltpu.VMEM)
    dma = pltpu.SemaphoreType.DMA
    return pl.pallas_call(
        kernel,
        out_shape=(
            jax.ShapeDtypeStruct((CH, ROWS, COLS), BF16),
            jax.ShapeDtypeStruct((3, 3, PART, CH), BF16),
            jax.ShapeDtypeStruct((CH, ROWS, COLS), BF16),
        ),
        in_specs=[vmem] * 6,
        out_specs=(vmem,) * 3,
        scratch_shapes=[
            pltpu.VMEM((ALL, LANES), BF16),
            pltpu.VMEM((ALL, LANES), BF16),
            pltpu.VMEM((ALL, LANES), BF16),
            pltpu.VMEM((2, 3 * CH, BLOCK), F32),
            pltpu.VMEM((CH, CELLS), F32),
            pltpu.VMEM((3 * CH, CELLS), BF16),
            pltpu.VMEM((CHANS, CH, 10 * CH), BF16),
            pltpu.VMEM((CHANS, CH, 10 * CH), BF16),
            pltpu.VMEM((10 * CH, ALL), BF16),
            pltpu.VMEM((TILES, PACK, 128), BF16),
            pltpu.VMEM((TILES, PACK, 128), BF16),
            pltpu.VMEM((ROWS * CH, TILES * CAP), BF16),
            pltpu.VMEM((2, 3, 96, ALL), BF16),
            pltpu.VMEM((3, 3, 96, ALL), BF16),
            pltpu.VMEM((3, 96, ALL), BF16),
            pltpu.VMEM((3, 3, 96, ALL), BF16),
            pltpu.VMEM((3, 96, ALL), BF16),
            pltpu.VMEM((3, 96, 128), BF16),
            dma((3, 10)), dma((3, 10)), dma((3, 8)), dma((3, 8)), dma((3, 8)), dma((3, 8)),
            dma((TILES,)), dma((TILES,)), dma((CHANS,)), dma((CHANS,)), dma((4,)), dma((4,)),
            dma((2, 2)), dma((3, 2)), dma((2,)), dma((3, 2)), dma((4, 2)), dma((1,)),
        ],
        compiler_params=pltpu.CompilerParams(
            collective_id=0, has_side_effects=True, vmem_limit_bytes=56 * 1024 * 1024
        ),
    )(grid, grad_out, station_feats, marks, w1, w2)


def solution(mesh):
    return jax.shard_map(
        local,
        mesh=mesh,
        in_specs=(
            P("chan", "tile", None),
            P("chan", "tile"),
            P("tile", None),
            P("tile"),
            P("tile"),
            P(None, None, None, "chan"),
            P(None, None, None, "chan"),
            P("chan", "tile", None),
        ),
        out_specs=(P("chan", "tile", None), P(None, None, "tile", "chan"), P("chan", "tile", None)),
        check_vma=False,
    )
```

profile of v0, /device:TPU:5, one launch (start us, length us, event | category | flops | bytes accessed | tf_op | source)
XLA Modules:
  0.0 92.2 jit_solution(3303046687614469458)
XLA Ops:
  0.6 0.0 copy-start.4
  0.6 0.0 copy-start.3
  0.7 0.0 copy-start.2
  0.7 0.1 pad.3.clone
  0.7 0.6 copy-done.4
  1.3 0.0 copy-done.3
  1.3 0.0 copy-done.2
  1.3 0.7 add_add_fusion.marks_ref
  2.0 86.8 %shard_map.103 = (bf16[64,16,256]{2,1,0:T(8,128)(2,1)}, bf16[3,3,32,64]{3,2,1,0:T(8,128)(2,1)}, bf16[64,16,256]{2,1,0:T(8,128)(2,1)}) custom-call(bf16[64,16,256]{2,1,0:T(8,128)(2,1)} %grid_ref.1, bf16[64,16,256]{2,1,0:T(8,128)(2,1)} %gout_ref.1, bf16[64,512]{1,0:T(8,128)(2,1)} %feats_ref.1, s32[8,512]{1,0:T(8,128)} %add_add_fusion.marks_ref, ...), custom_call_target="tpu_custom_call" | custom-call | tf_op jit(solution)/shard_map/pallas_call | solution.py:575
  88.8 0.0 copy-start.1
  88.8 0.0 copy-start
  88.8 1.9 %copy.14 = bf16[64,16,256]{2,1,0:T(8,128)(2,1)} copy(bf16[64,16,256]{2,1,0:T(8,128)(2,1)} %get-tuple-element.6) | data formatting | bytes 1048576
  90.7 0.0 copy-done.1
  90.8 0.6 copy.15
  91.4 0.0 copy-done
  91.4 0.8 copy.16
  (1 shorter events, 0.0 us)
Async XLA Ops:
  0.6 0.7 copy-start.4
  0.6 0.7 copy-start.3
  0.7 0.7 copy-start.2
  88.8 2.0 %copy-start.1 = (bf16[3,3,32,64]{3,2,1,0:T(8,128)(2,1)S(1)}, bf16[3,3,32,64]{3,2,1,0:T(8,128)(2,1)}, u32[]{:S(2)}) copy-start(bf16[3,3,32,64]{3,2,1,0:T(8,128)(2,1)} %get-tuple-element.7) | copy-start | bytes 110596
  88.8 2.6 %copy-start = (bf16[64,16,256]{2,1,0:T(8,128)(2,1)S(1)}, bf16[64,16,256]{2,1,0:T(8,128)(2,1)}, u32[]{:S(2)}) copy-start(bf16[64,16,256]{2,1,0:T(8,128)(2,1)} %get-tuple-element.8) | copy-start | bytes 1572868
where the time goes:
time: 92.4 us; the launch traced here: 92.2 us
  Pallas kernels  86.8 us (94%)
  local copies, waits for them, and re-layouts  4.04 us (4%)
    pallas_call x1, Pallas kernels, local(): pl.pallas_call(kernel, out_shape=(jax.ShapeDtypeStruct((CH, ROWS, COLS),...  86.8 us
    unnamed x13, local copies, waits for them, and re-layouts  3.97 us

commit v1 on v0

--- a/solution.py
+++ b/solution.py
@@ -20,7 +20,7 @@
 ALL = CH * CHANS
 SHARD = 512
 CAP = 64
-PACK = 80
+PACK = 96
 PART = 32
 NT = (((1,), (1,)), ((), ()))
 
@@ -40,9 +40,9 @@
 
 
 def kernel(
-    grid_ref, gout_ref, feats_ref, marks_ref, w1_ref, w2_ref,
+    feats_ref, owner_ref, valid_ref, cell_ref, gout_hbm, grid_hbm, w1_hbm, w2_hbm,
     out_ref, gw_ref, gh_ref,
-    ga, aa, ha, zbuf, hidden_pre, h3, b2, wb, wbt, packed, landed, masked,
+    gout_ref, grid_ref, w1_ref, w2_ref, in_sem, ga, aa, ha, zbuf, hidden_pre, h3, b2, wb, wbt, packed, landed, masked,
     gw_out, gw_one, gw_mid, gw_two, gw_fin, gw_land,
     x_send, x_recv, e_send, e_recv, d_send, d_recv, s_send, s_recv, w_send, w_recv, v_send, v_recv,
     one_send, one_recv, two_send, two_recv, three_send, three_recv,
@@ -58,6 +58,15 @@
     sibling = (tile, x * 2 + (1 - core))
     has_up, has_down = tile > 0, tile < TILES - 1
 
+    inward = [
+        pltpu.make_async_copy(src, dst, in_sem.at[k])
+        for k, (src, dst) in enumerate(
+            ((gout_hbm, gout_ref), (w2_hbm, w2_ref), (grid_hbm, grid_ref), (w1_hbm, w1_ref))
+        )
+    ]
+    for copy in inward:
+        copy.start()
+
     barrier = pltpu.get_barrier_semaphore()
     for step in range(1, TILES):
         pl.semaphore_signal(barrier, inc=1, device_id=((tile + step) % TILES, chan), device_id_type=MESH)
@@ -71,8 +80,8 @@
         return pl.ds(pl.multiple_of(chip * (2 * CH), 2 * CH), 2 * CH)
 
     own = rows_of(x, core)
-    halves = (pl.ds(COLS, BLOCK), pl.ds(COLS + BLOCK, BLOCK))
     quarters = [pl.ds(COLS + q * 1024, 1024) for q in range(4)]
+    middle = pl.ds(COLS + 1024, BLOCK)
     top, bottom = pl.ds(0, COLS), pl.ds(COLS + CELLS, COLS)
     first, last = pl.ds(COLS, COLS), pl.ds(CELLS, COLS)
     inner = pl.ds(COLS, CELLS)
@@ -82,17 +91,12 @@
             src_ref=src, dst_ref=dst, send_sem=send, recv_sem=recv, device_id=device, device_id_type=MESH
         )
 
+    outer = (quarters[0], quarters[3], middle)
     x_table = (
-        (0, halves[0], 0, CH, True, 1),
-        (0, halves[1], 0, CH, True, 1),
-        (0, halves[0], 0, CH, False, 2),
-        (0, halves[1], 0, CH, False, 2),
-        (1, halves[0], 0, CH // 2, True, 3),
-        (1, quarters[3], 0, CH // 2, True, 3),
-        (1, quarters[2], 0, CH // 2, True, 3),
-        (2, halves[0], CH // 2, CH // 2, False, 3),
-        (2, quarters[3], CH // 2, CH // 2, False, 3),
-        (2, quarters[2], CH // 2, CH // 2, False, 3),
+        *((0, lanes, 0, CH, True, 1) for lanes in outer),
+        *((0, lanes, 0, CH, False, 2) for lanes in outer),
+        *((1, lanes, 0, CH // 2, True, 3) for lanes in outer),
+        *((2, lanes, CH // 2, CH // 2, False, 3) for lanes in outer),
     )
 
     def x_copy(f, k, arriving=False):
@@ -122,11 +126,11 @@
         (0, pl.ds(0, LANES)),
         (1, pl.ds(0, LANES)),
         (2, pl.ds(0, LANES)),
-        (3, halves[0]),
+        (3, quarters[0]),
         (3, quarters[3]),
-        (3, quarters[2]),
         (3, top),
         (3, bottom),
+        (3, middle),
     )
 
     def d_copy(f, k, arriving=False):
@@ -134,66 +138,62 @@
         place = bufs[f].at[rows_of(chips[j], 1 - core if arriving else core), lanes]
         return remote(place, place, d_send.at[f, k], d_recv.at[f, k], sibling)
 
-    def own_start(f, half):
-        x_copy(f, half).start()
-        x_copy(f, 2 + half).start()
-        e_start(f, 0, half)
+    def own_start(f, second):
+        if second:
+            x_copy(f, 2).start()
+            x_copy(f, 5).start()
+            return
+        for k in (0, 3, 1, 4):
+            x_copy(f, k).start()
+        e_start(f, 0, 0)
+        e_start(f, 0, 1)
 
     def pass_on(f, j):
         e_wait_recv(f, j, 1)
         e_wait_recv(f, j, 0)
         d_copy(f, j).start()
 
-    def forward(f, ks):
-        for k in ks:
-            x_copy(f, k).start()
-
-    def near(f, onward):
-        x_copy(f, 0, True).wait_recv()
-        if onward:
-            forward(f, (4,))
-        e_start(f, 1, 0)
-        x_copy(f, 2, True).wait_recv()
-        if onward:
-            forward(f, (7,))
-        e_start(f, 2, 0)
-        x_copy(f, 1, True).wait_recv()
-        if onward:
-            forward(f, (5, 6))
-        e_start(f, 1, 1)
-        x_copy(f, 3, True).wait_recv()
-        if onward:
-            forward(f, (8, 9))
-        e_start(f, 2, 1)
-
-    def far(f):
-        x_copy(f, 4, True).wait_recv()
-        x_copy(f, 7, True).wait_recv()
-        e_start(f, 3, 0)
-        d_copy(f, 3).start()
-        x_copy(f, 5, True).wait_recv()
+    def near_first(f, onward):
+        for part in range(2):
+            for side in range(2):
+                x_copy(f, 3 * side + part, True).wait_recv()
+                if onward:
+                    x_copy(f, 6 + 3 * side + part).start()
+                e_start(f, 1 + side, part)
+
+    def near_second(f, onward):
+        for side in range(2):
+            x_copy(f, 3 * side + 2, True).wait_recv()
+            if onward:
+                x_copy(f, 8 + 3 * side).start()
+
+    def far_first(f):
+        for part in range(2):
+            x_copy(f, 6 + part, True).wait_recv()
+            x_copy(f, 9 + part, True).wait_recv()
+            e_start(f, 3, part)
+            d_copy(f, 3 + part).start()
+
+    def far_second(f):
         x_copy(f, 8, True).wait_recv()
-        e_start(f, 3, 1)
-        d_copy(f, 4).start()
-        x_copy(f, 6, True).wait_recv()
-        x_copy(f, 9, True).wait_recv()
-        d_copy(f, 5).start()
+        x_copy(f, 11, True).wait_recv()
+        d_copy(f, 7).start()
 
     def far_edges(f):
         e_wait_recv(f, 3, 1)
+        d_copy(f, 5).start()
+        e_wait_recv(f, 3, 0)
         d_copy(f, 6).start()
-        e_wait_recv(f, 3, 0)
-        d_copy(f, 7).start()
 
     def d_wait(f, j):
         for k in range(len(d_table)):
             if d_table[k][0] == j:
                 d_copy(f, k, True).wait_recv()
 
-    def products(buf, weights, pairs, block):
+    def products(buf, weights, pairs, start, size):
         total = None
         for r in range(3):
-            lanes = pl.ds(pl.multiple_of(block * BLOCK + r * COLS, COLS), BLOCK)
+            lanes = pl.ds(start + r * COLS, size)
             taps = pl.ds(r * 3 * CH, 3 * CH)
             if pairs is None:
                 lhs, rhs = weights[taps, :], buf[:, lanes]
@@ -207,18 +207,13 @@
         return total
 
     def conv_pass(buf, weights, pairs, start):
-        @pl.loop(0, 2)
-        def _(block):
-            terms = products(buf, weights, pairs, block)
-            zbuf[block] = terms if start else zbuf[block] + terms
-
-    def block_lanes(block, skip=0):
-        return pl.ds(pl.multiple_of(block * BLOCK + skip, COLS), BLOCK)
-
-    def block_rows(block):
-        return pl.ds(pl.multiple_of(block * (ROWS // 2), ROWS // 2), ROWS // 2)
+        for block in range(2):
+            lanes = pl.ds(block * BLOCK, BLOCK)
+            terms = products(buf, weights, pairs, block * BLOCK, BLOCK)
+            zbuf[:, lanes] = terms if start else zbuf[:, lanes] + terms
 
     with jax.named_scope("prepare"):
+        inward[0].wait()
         ga[own, inner] = gout_ref[...].reshape(CH, CELLS)
         for buf in bufs:
             for chip in chips:
@@ -230,7 +225,14 @@
                 def _(buf=buf, chip=chip):
                     buf[rows_of(chip, core), bottom] = jnp.zeros((CH, COLS), BF16)
 
-        marks = marks_ref[...]
+    with jax.named_scope("barrier_wait"):
+        pl.semaphore_wait(barrier, TILES + CHANS - 2)
+    with jax.named_scope("first_sends"):
+        own_start(G, 0)
+        own_start(G, 1)
+
+    with jax.named_scope("stations"):
+        marks = jnp.concatenate([owner_ref[...], valid_ref[...], jnp.zeros((6, SHARD), jnp.int32)], axis=0)
         columns = marks.astype(F32).T
         owners, usable = columns[:, 0:1].astype(jnp.int32), columns[:, 1:2] == 1.0
         tile_of = lax.broadcasted_iota(jnp.int32, (SHARD, 128), 1)
@@ -238,21 +240,22 @@
         lower = lax.broadcasted_iota(jnp.int32, (SHARD, SHARD), 0) >= lax.broadcasted_iota(jnp.int32, (SHARD, SHARD), 1)
         counts = jnp.dot(jnp.where(lower, 1.0, 0.0).astype(BF16), named.astype(BF16), preferred_element_type=F32)
         rank = jnp.sum(counts * named, axis=1, keepdims=True).astype(jnp.int32) - 1
-        slot = jnp.where(usable, owners * 128 + (tile % 2) * CAP + rank, -1)
-        cells = marks[2:3]
+        slot = jnp.where(usable, owners * CAP + rank, -1)
+        cells = cell_ref[...]
         sub = lax.broadcasted_iota(jnp.int32, (PACK - CH, SHARD), 0)
         places = jnp.where(sub == 0, cells // COLS, jnp.where(sub == 1, cells % COLS, 0))
         rowed = jnp.concatenate([feats_ref[...], places.astype(F32).astype(BF16)], axis=0)
-        for part in range(4):
+        lane = lax.broadcasted_iota(jnp.int32, (PACK // 2, 128), 1)
+        for part in range(2):
             number = lax.broadcasted_iota(jnp.int32, (SHARD, 512), 1) + part * 512
             chosen = jnp.where(slot == number, 1.0, 0.0).astype(BF16)
-            sent = jnp.dot(rowed, chosen, preferred_element_type=F32).astype(BF16)
+            sent = jnp.dot(rowed, chosen, preferred_element_type=F32)
             for k in range(4):
-                packed[part * 4 + k] = sent[:, k * 128 : (k + 1) * 128]
+                upper, lower = sent[: PACK // 2, k * 128 : (k + 1) * 128], sent[PACK // 2 :, k * 128 : (k + 1) * 128]
+                to = 2 * (part * 4 + k)
+                packed[to] = jnp.where(lane < CAP, upper, pltpu.roll(lower, CAP, 1)).astype(BF16)
+                packed[to + 1] = jnp.where(lane < CAP, pltpu.roll(upper, CAP, 1), lower).astype(BF16)
         landed[tile] = packed[tile]
-
-    with jax.named_scope("barrier_wait"):
-        pl.semaphore_wait(barrier, TILES + CHANS - 2)
 
     def s_copy(step, arriving=False):
         other = (tile + step) % TILES
@@ -275,13 +278,11 @@
         place = wb.at[:, pl.ds(pl.multiple_of(quarter * 16, 16), 16)]
         return remote(place, place, v_send.at[step], v_recv.at[step], (other, chan))
 
-    with jax.named_scope("first_sends"):
-        for step in range(1, TILES):
-            s_copy(step).start()
-        own_start(G, 0)
-        own_start(G, 1)
+    for step in range(1, TILES):
+        s_copy(step).start()
 
     with jax.named_scope("weight_pieces"):
+        inward[1].wait()
         lane = lax.broadcasted_iota(jnp.int32, (CH, 128), 1)
         for chip in range(4):
             taps = [w2_ref[pl.ds((8 - n) * CH, CH), pl.ds(chip * 128, 128)].astype(F32) for n in range(9)]
@@ -301,78 +302,96 @@
         for step in range(1, TILES):
             s_copy(step, True).wait_recv()
     with jax.named_scope("assimilate"):
-        stations = jnp.concatenate([landed[2 * k] + landed[2 * k + 1] for k in range(TILES // 2)], axis=1)
+        lane = lax.broadcasted_iota(jnp.int32, (PACK // 2, 128), 1)
+        slabs = []
+        for k in range(TILES // 2):
+            even, odd = landed[2 * k].astype(F32), landed[2 * k + 1].astype(F32)
+            upper = jnp.where(lane < CAP, even, pltpu.roll(odd, CAP, 1))
+            lower = jnp.where(lane < CAP, pltpu.roll(even, CAP, 1), odd)
+            slabs.append(jnp.concatenate([upper, lower], axis=0))
+        stations = jnp.concatenate(slabs, axis=1)
         slots = stations.shape[1]
-        station_row = stations[CH : CH + 1].astype(F32)
-        station_col = stations[CH + 1 : CH + 2].astype(F32)
+        station_row, station_col = stations[CH : CH + 1], stations[CH + 1 : CH + 2]
         spread = lax.broadcasted_iota(jnp.int32, (COLS, slots), 0).astype(F32)
         col_hot = jnp.where(station_col == spread, 1.0, 0.0).astype(BF16)
-        features = stations[:CH].astype(F32)
+        features = stations[:CH]
         for i in range(ROWS):
             masked[pl.ds(i * CH, CH), :] = jnp.where(station_row == float(i), features, 0.0).astype(BF16)
+        inward[2].wait()
         background = grid_ref[...].reshape(CH, CELLS)
-        for half in range(2):
-            rows = pl.ds(half * 512, 512)
+        for number, quarter in enumerate((0, 3, 1, 2)):
+            rows = pl.ds(quarter * 256, 256)
             sums = lax.dot_general(masked[rows, :], col_hot, NT, preferred_element_type=F32)
-            for k in range(8):
-                i = half * 8 + k
+            for k in range(4):
+                i = quarter * 4 + k
                 value = background[:, i * COLS : (i + 1) * COLS].astype(F32) + sums[k * CH : (k + 1) * CH]
                 aa[own, pl.ds((i + 1) * COLS, COLS)] = value.astype(BF16)
-            own_start(A, half)
+            if number % 2:
+                own_start(A, number // 2)
 
     with jax.named_scope("pass_on_0"):
         pass_on(G, 0)
+        pass_on(A, 0)
+    with jax.named_scope("wait_A0"):
+        d_wait(A, 0)
+    with jax.named_scope("conv1_pass1"):
+        inward[3].wait()
+        conv_pass(aa, w1_ref, [chips[0]], True)
+    with jax.named_scope("weights_round"):
         for step in range(1, CHANS):
             w_copy(step, True).wait_recv()
         for step in range(1, 4):
             v_copy(step).start()
-        pass_on(A, 0)
-    with jax.named_scope("wait_A0"):
-        d_wait(A, 0)
-    with jax.named_scope("conv1_pass1"):
-        conv_pass(aa, w1_ref, [chips[0]], True)
-    with jax.named_scope("near_G"):
-        near(G, False)
-        pass_on(G, 1)
-        pass_on(G, 2)
-    with jax.named_scope("turn_weights"):
-        for step in range(1, 4):
-            v_copy(step, True).wait_recv()
-        for s in range(CHANS // 2):
-            two = jnp.concatenate([wb[2 * s], wb[2 * s + 1]], axis=0).astype(F32)
-            wbt[:, pl.ds(s * 128, 128)] = two.T.astype(BF16)
-    with jax.named_scope("near_A"):
-        near(A, True)
+    with jax.named_scope("near_G1"):
+        near_first(G, False)
+    with jax.named_scope("near_A1"):
+        near_first(A, True)
+    with jax.named_scope("near_G2"):
+        near_second(G, False)
+    with jax.named_scope("near_A2"):
+        near_second(A, True)
+    with jax.named_scope("pass_on_A12"):
         pass_on(A, 1)
         pass_on(A, 2)
+    with jax.named_scope("far_A1"):
+        far_first(A)
     with jax.named_scope("wait_A12"):
         d_wait(A, 1)
         d_wait(A, 2)
     with jax.named_scope("conv1_pass2"):
         conv_pass(aa, w1_ref, [chips[1], chips[2]], False)
-    with jax.named_scope("far_A"):
-        far(A)
-        forward(G, (4, 7, 5, 8, 6, 9))
+    with jax.named_scope("far_A2"):
+        far_second(A)
+        for k in (6, 9, 7, 10, 8, 11):
+            x_copy(G, k).start()
+    with jax.named_scope("far_A_edges"):
         far_edges(A)
+        pass_on(G, 1)
+        pass_on(G, 2)
     with jax.named_scope("wait_A3"):
         d_wait(A, 3)
     with jax.named_scope("conv1_pass3"):
-        for half in range(2):
-            value = neighbour_sum(zbuf[half] + products(aa, w1_ref, [chips[3]], half))
-            hidden_pre[:, block_lanes(half)] = value
+        for number, (start, size) in enumerate(((0, 1024), (3072, 1024), (1024, BLOCK))):
+            lanes = pl.ds(start, size)
+            value = neighbour_sum(zbuf[:, lanes] + products(aa, w1_ref, [chips[3]], start, size))
+            hidden_pre[:, lanes] = value
             hidden = value * (1.0 / (1.0 + jnp.exp(-value)))
-            ha[own, block_lanes(half, COLS)] = hidden.astype(BF16)
-            own_start(H, half)
+            ha[own, pl.ds(start + COLS, size)] = hidden.astype(BF16)
+            if number:
+                own_start(H, number - 1)
+
+    groups = ((0, 1, 2), (3,))
+    group_lanes = (pl.ds(0, 384), pl.ds(384, 128))
 
     def weight_terms(group):
         for r in range(3):
             lanes = pl.ds((2 - r) * COLS, CELLS)
-            against = jnp.concatenate([ga[pair_of(chips[2 * group + k]), lanes] for k in range(2)], axis=0)
+            against = [ga[pair_of(chips[j]), lanes] for j in groups[group]]
+            against = against[0] if len(against) == 1 else jnp.concatenate(against, axis=0)
             term = lax.dot_general(h3[...], against, NT, preferred_element_type=F32).astype(BF16)
             for part in range(2):
-                gw_out[part, r, :, pl.ds(group * 256, 256)] = term[part * 96 : (part + 1) * 96]
-
-    group_lanes = (pl.ds(0, 256), pl.ds(256, 256))
+                gw_out[part, r, :, group_lanes[group]] = term[part * 96 : (part + 1) * 96]
+
     collects = z // 2 == core
     owns = collects & (y == x)
 
@@ -431,9 +450,12 @@
             total = gw_mid[:, :, lanes].astype(F32)
             for slot in range(3):
                 total = total + gw_two[slot, :, :, lanes].astype(F32)
-            gw_fin[:, :, lanes] = total.astype(BF16)
-            for k in range(2):
-                j = 2 * group + k
+            lane = lax.broadcasted_iota(jnp.int32, (144, 128), 1)
+            for k, j in enumerate(groups[group]):
+                both = total[:, :, k * 128 : (k + 1) * 128].reshape(288, 128)
+                upper, lower = both[:144], both[144:]
+                gw_fin[j, 0] = jnp.where(lane < CH, upper, pltpu.roll(lower, CH, 1)).astype(BF16)
+                gw_fin[j, 1] = jnp.where(lane < CH, pltpu.roll(upper, CH, 1), lower).astype(BF16)
                 for which in range(2):
                     if j == 0:
                         @pl.when(core != which)
@@ -442,11 +464,11 @@
                     else:
                         three_copy(j, which).start()
             if group == 0:
-                gw_land[...] = gw_fin[:, :, pl.ds(0, 128)]
+                gw_land[...] = gw_fin[0, core]
 
     def three_copy(j, which):
         return remote(
-            gw_fin.at[:, :, pl.ds(j * 128, 128)],
+            gw_fin.at[j, which],
             gw_land,
             three_send.at[j, which],
             three_recv.at[0],
@@ -467,59 +489,73 @@
         one_start(0)
     with jax.named_scope("pass_on_H0"):
         pass_on(H, 0)
-    with jax.named_scope("far_G"):
-        far(G)
-        far_edges(G)
-        d_wait(G, 3)
-    with jax.named_scope("weight_terms_1"):
-        weight_terms(1)
-        one_start(1)
-    with jax.named_scope("grad_hidden"):
-        @pl.loop(0, 2)
-        def _(block):
-            grad_act = neighbour_sum(products(ga, wbt, None, block))
-            value = hidden_pre[:, block_lanes(block)]
-            s = 1.0 / (1.0 + jnp.exp(-value))
-            result = (grad_act * s * (1.0 + value * (1.0 - s))).astype(BF16)
-            gh_ref[:, block_rows(block), :] = result.reshape(CH, ROWS // 2, COLS)
-    with jax.named_scope("near_H"):
-        near(H, True)
-        pass_on(H, 1)
-        pass_on(H, 2)
-    with jax.named_scope("collect_0"):
-        collect(0)
     with jax.named_scope("conv2_pass1"):
         d_wait(H, 0)
         conv_pass(ha, w2_ref, [chips[0]], True)
+    with jax.named_scope("near_H1"):
+        near_first(H, True)
+    with jax.named_scope("far_G"):
+        far_first(G)
+        far_second(G)
+        far_edges(G)
+    with jax.named_scope("collect_0"):
+        collect(0)
+    with jax.named_scope("weight_terms_1"):
+        d_wait(G, 3)
+        weight_terms(1)
+        one_start(1)
+    with jax.named_scope("near_H2"):
+        near_second(H, True)
+        pass_on(H, 1)
+        pass_on(H, 2)
+    with jax.named_scope("turn_weights"):
+        for step in range(1, 4):
+            v_copy(step, True).wait_recv()
+        for s in range(CHANS // 2):
+            two = jnp.concatenate([wb[2 * s], wb[2 * s + 1]], axis=0).astype(F32)
+            wbt[:, pl.ds(s * 128, 128)] = two.T.astype(BF16)
+    with jax.named_scope("far_H1"):
+        far_first(H)
     with jax.named_scope("collect_1"):
         collect(1)
+    with jax.named_scope("grad_hidden"):
+        for block in range(2):
+            lanes = pl.ds(block * BLOCK, BLOCK)
+            grad_act = neighbour_sum(products(ga, wbt, None, block * BLOCK, BLOCK))
+            value = hidden_pre[:, lanes]
+            s = 1.0 / (1.0 + jnp.exp(-value))
+            result = (grad_act * s * (1.0 + value * (1.0 - s))).astype(BF16)
+            gh_ref[:, block * 8 : block * 8 + 8, :] = result.reshape(CH, 8, COLS)
     with jax.named_scope("conv2_pass2"):
         d_wait(H, 1)
         d_wait(H, 2)
         conv_pass(ha, w2_ref, [chips[1], chips[2]], False)
-    with jax.named_scope("far_H"):
-        far(H)
+    with jax.named_scope("finish_0"):
+        finish(0)
+    with jax.named_scope("finish_1"):
+        finish(1)
+    with jax.named_scope("far_H2"):
+        far_second(H)
+    with jax.named_scope("far_H_edges"):
         far_edges(H)
-    with jax.named_scope("finish"):
-        finish(0)
-        finish(1)
     with jax.named_scope("wait_H3"):
         d_wait(H, 3)
     with jax.named_scope("conv2_pass3"):
-        for half in range(2):
-            branch = neighbour_sum(zbuf[half] + products(ha, w2_ref, [chips[3]], half))
-            result = (aa[own, block_lanes(half, COLS)].astype(F32) + branch).astype(BF16)
-            out_ref[:, half * (ROWS // 2) : (half + 1) * (ROWS // 2), :] = result.reshape(CH, ROWS // 2, COLS)
+        for block in range(2):
+            lanes = pl.ds(block * BLOCK, BLOCK)
+            branch = neighbour_sum(zbuf[:, lanes] + products(ha, w2_ref, [chips[3]], block * BLOCK, BLOCK))
+            result = (aa[own, pl.ds(block * BLOCK + COLS, BLOCK)].astype(F32) + branch).astype(BF16)
+            out_ref[:, block * 8 : block * 8 + 8, :] = result.reshape(CH, 8, COLS)
     with jax.named_scope("grad_weight"):
         @pl.when(jnp.logical_not(owns))
         def _():
             remote(gw_land, gw_land, three_recv.at[0], three_recv.at[0], (tile, chan)).wait_recv()
 
-        for r in range(3):
-            piece = gw_land[r].astype(F32)
-            piece = jnp.where(core == 0, piece, pltpu.roll(piece, CH, 1))[:, :CH].astype(BF16)
-            for q in range(3):
-                gw_ref[r, q] = piece[q * PART : (q + 1) * PART]
+        piece = gw_land[...].astype(F32)
+        sides = (piece[:, :CH].astype(BF16), pltpu.roll(piece, CH, 1)[:, :CH].astype(BF16))
+        for n in range(18):
+            rows = sides[n // 9][(n % 9) * 16 : (n % 9) * 16 + 16]
+            gw_ref[n // 6, n % 6 // 2, pl.ds(n % 2 * 16, 16), :] = rows
 
     with jax.named_scope("sends_done"):
         for f in (G, A, H):
@@ -564,50 +600,86 @@
                         three_copy(j, which).wait_send()
 
 
+def hand_over(out_from, gw_from, gh_from, out_to, gw_to, gh_to, out_via, gw_via, gh_via, sems):
+    parts = [pl.ds(k * 16, 16) for k in range(4)]
+    ways = [(gw_from, gw_via, gw_to)]
+    for part in parts:
+        ways.append((out_from.at[part], out_via.at[part], out_to.at[part]))
+        ways.append((gh_from.at[part], gh_via.at[part], gh_to.at[part]))
+    inward = [pltpu.make_async_copy(src, via, sems.at[0, k]) for k, (src, via, _) in enumerate(ways)]
+    outward = [pltpu.make_async_copy(via, dst, sems.at[1, k]) for k, (_, via, dst) in enumerate(ways)]
+    for copy in inward:
+        copy.start()
+    for arrive, leave in zip(inward, outward):
+        arrive.wait()
+        leave.start()
+    for copy in outward:
+        copy.wait()
+
+
 def local(grid, station_feats, owner_tile, station_cell, valid, conv_first, conv_second, grad_out):
     w1 = conv_first.transpose(0, 1, 3, 2).reshape(9 * CH, ALL)
     w2 = conv_second.transpose(0, 1, 3, 2).reshape(9 * CH, ALL)
-    marks = jnp.concatenate(
-        [owner_tile.reshape(1, SHARD), valid.reshape(1, SHARD), station_cell.reshape(1, SHARD), jnp.zeros((5, SHARD), jnp.int32)]
-    )
+    whole = pl.BlockSpec(memory_space=pl.ANY)
     vmem = pl.BlockSpec(memory_space=pltpu.VMEM)
     dma = pltpu.SemaphoreType.DMA
-    return pl.pallas_call(
+    results = pl.pallas_call(
         kernel,
         out_shape=(
             jax.ShapeDtypeStruct((CH, ROWS, COLS), BF16),
             jax.ShapeDtypeStruct((3, 3, PART, CH), BF16),
             jax.ShapeDtypeStruct((CH, ROWS, COLS), BF16),
         ),
-        in_specs=[vmem] * 6,
+        in_specs=[vmem] * 4 + [whole] * 4,
         out_specs=(vmem,) * 3,
         scratch_shapes=[
+            pltpu.VMEM((CH, ROWS, COLS), BF16),
+            pltpu.VMEM((CH, ROWS, COLS), BF16),
+            pltpu.VMEM((9 * CH, ALL), BF16),
+            pltpu.VMEM((9 * CH, ALL), BF16),
+            dma((4,)),
             pltpu.VMEM((ALL, LANES), BF16),
             pltpu.VMEM((ALL, LANES), BF16),
             pltpu.VMEM((ALL, LANES), BF16),
-            pltpu.VMEM((2, 3 * CH, BLOCK), F32),
+            pltpu.VMEM((3 * CH, CELLS), F32),
             pltpu.VMEM((CH, CELLS), F32),
             pltpu.VMEM((3 * CH, CELLS), BF16),
             pltpu.VMEM((CHANS, CH, 10 * CH), BF16),
             pltpu.VMEM((CHANS, CH, 10 * CH), BF16),
             pltpu.VMEM((10 * CH, ALL), BF16),
-            pltpu.VMEM((TILES, PACK, 128), BF16),
-            pltpu.VMEM((TILES, PACK, 128), BF16),
+            pltpu.VMEM((TILES, PACK // 2, 128), BF16),
+            pltpu.VMEM((TILES, PACK // 2, 128), BF16),
             pltpu.VMEM((ROWS * CH, TILES * CAP), BF16),
             pltpu.VMEM((2, 3, 96, ALL), BF16),
             pltpu.VMEM((3, 3, 96, ALL), BF16),
             pltpu.VMEM((3, 96, ALL), BF16),
             pltpu.VMEM((3, 3, 96, ALL), BF16),
-            pltpu.VMEM((3, 96, ALL), BF16),
-            pltpu.VMEM((3, 96, 128), BF16),
-            dma((3, 10)), dma((3, 10)), dma((3, 8)), dma((3, 8)), dma((3, 8)), dma((3, 8)),
+            pltpu.VMEM((4, 2, 144, 128), BF16),
+            pltpu.VMEM((144, 128), BF16),
+            dma((3, 12)), dma((3, 12)), dma((3, 8)), dma((3, 8)), dma((3, 8)), dma((3, 8)),
             dma((TILES,)), dma((TILES,)), dma((CHANS,)), dma((CHANS,)), dma((4,)), dma((4,)),
             dma((2, 2)), dma((3, 2)), dma((2,)), dma((3, 2)), dma((4, 2)), dma((1,)),
         ],
         compiler_params=pltpu.CompilerParams(
             collective_id=0, has_side_effects=True, vmem_limit_bytes=56 * 1024 * 1024
         ),
-    )(grid, grad_out, station_feats, marks, w1, w2)
+    )(
+        station_feats,
+        owner_tile.reshape(1, SHARD),
+        valid.reshape(1, SHARD),
+        station_cell.reshape(1, SHARD),
+        grad_out,
+        grid,
+        w1,
+        w2,
+    )
+    return pl.pallas_call(
+        hand_over,
+        out_shape=tuple(jax.ShapeDtypeStruct(result.shape, result.dtype) for result in results),
+        in_specs=[whole] * 3,
+        out_specs=(whole,) * 3,
+        scratch_shapes=[*(pltpu.VMEM(result.shape, BF16) for result in results), dma((2, 9))],
+    )(*results)
 
 
 def solution(mesh):

time: 92.4 us -> 81.5 us (0.88); the launches traced: 92.2 us -> 80.2 us
  Pallas kernels: 86.8 us -> 79.4 us
  local copies, waits for them, and re-layouts: 4.04 us -> 0 us
    pallas_call x1, Pallas kernels: 86.8 us -> 77.2 us  [local(): pl.pallas_call(kernel, out_shape=(jax.ShapeDtypeStruct((CH, ROWS, COLS),...]
    unnamed x13 -> x0, local copies, waits for them, and re-layouts: 3.97 us -> none
    pallas_call x0 -> x1, Pallas kernels: none -> 2.14 us  [local(): pl.pallas_call(hand_over, out_shape=tuple((jax.ShapeDtypeStruct(result.sh...]
where the time goes in v1:
time: 81.5 us; the launch traced here: 80.2 us
  Pallas kernels  79.4 us (97%)
    pallas_call x1, Pallas kernels, local(): pl.pallas_call(kernel, out_shape=(jax.ShapeDtypeStruct((CH, ROWS, COLS),...  77.2 us
    pallas_call x1, Pallas kernels, local(): pl.pallas_call(hand_over, out_shape=tuple((jax.ShapeDtypeStruct(result.sh...  2.14 us

profile of v1, /device:TPU:5, one launch (start us, length us, event | category | flops | bytes accessed | tf_op | source)
XLA Modules:
  0.0 80.2 jit_solution(12421252386950192540)
XLA Ops:
  0.6 77.2 %shard_map.103 = (bf16[64,16,256]{2,1,0:T(8,128)(2,1)}, bf16[3,3,32,64]{3,2,1,0:T(8,128)(2,1)}, bf16[64,16,256]{2,1,0:T(8,128)(2,1)}) custom-call(bf16[64,512]{1,0:T(8,128)(2,1)} %feats_ref.1, s32[1,512]{1,0:T(1,128)} %bitcast.11, s32[1,512]{1,0:T(1,128)} %bitcast.12, s32[1,512]{1,0:T(1,128)} %bitcast.13, bf16[64,16,256]{2,1,0:T(8,128)(2,1)} %gout_hbm.1, ...), custom_call_target="tpu_custom_call" | custom-call | tf_op jit(solution)/shard_map/pallas_call | solution.py:626
  77.9 2.1 %shard_map.104 = (bf16[64,16,256]{2,1,0:T(8,128)(2,1)}, bf16[3,3,32,64]{3,2,1,0:T(8,128)(2,1)}, bf16[64,16,256]{2,1,0:T(8,128)(2,1)}) custom-call(bf16[64,16,256]{2,1,0:T(8,128)(2,1)} %get-tuple-element.6.out_from, bf16[3,3,32,64]{3,2,1,0:T(8,128)(2,1)} %get-tuple-element.7.gw_from, bf16[64,16,256]{2,1,0:T(8,128)(2,1)} %get-tuple-element.8.gh_from), custom_call_target="tpu_custom_call" | custom-call | tf_op jit(solution)/shard_map/pallas_call | solution.py:676

commit v2 on v1

--- a/solution.py
+++ b/solution.py
@@ -42,7 +42,7 @@
 def kernel(
     feats_ref, owner_ref, valid_ref, cell_ref, gout_hbm, grid_hbm, w1_hbm, w2_hbm,
     out_ref, gw_ref, gh_ref,
-    gout_ref, grid_ref, w1_ref, w2_ref, in_sem, ga, aa, ha, zbuf, hidden_pre, h3, b2, wb, wbt, packed, landed, masked,
+    gout_ref, grid_ref, w1_ref, w2_ref, in_sem, ga, aa, ha, zbuf, hidden_pre, h3, b2, wb, wbt, packed, passing, landed, masked,
     gw_out, gw_one, gw_mid, gw_two, gw_fin, gw_land,
     x_send, x_recv, e_send, e_recv, d_send, d_recv, s_send, s_recv, w_send, w_recv, v_send, v_recv,
     one_send, one_recv, two_send, two_recv, three_send, three_recv,
@@ -68,8 +68,15 @@
         copy.start()
 
     barrier = pltpu.get_barrier_semaphore()
-    for step in range(1, TILES):
-        pl.semaphore_signal(barrier, inc=1, device_id=((tile + step) % TILES, chan), device_id_type=MESH)
+    across_up, across_down = has_up & (z == 0), has_down & (z == 3)
+    for step in range(1, 4):
+        for peer in (y * 4 + (z + step) % 4, (y + step) % 4 * 4 + z):
+            pl.semaphore_signal(barrier, inc=1, device_id=(peer, chan), device_id_type=MESH)
+    for across, peer in ((across_up, jnp.maximum(tile - 1, 0)), (across_down, jnp.minimum(tile + 1, TILES - 1))):
+        @pl.when(across)
+        def _(peer=peer):
+            pl.semaphore_signal(barrier, inc=1, device_id=(peer, chan), device_id_type=MESH)
+
     for step in range(1, CHANS):
         pl.semaphore_signal(barrier, inc=1, device_id=(tile, (chan + step) % CHANS), device_id_type=MESH)
 
@@ -122,16 +129,8 @@
         def _():
             e_copy(f, j, down, True).wait_recv()
 
-    d_table = (
-        (0, pl.ds(0, LANES)),
-        (1, pl.ds(0, LANES)),
-        (2, pl.ds(0, LANES)),
-        (3, quarters[0]),
-        (3, quarters[3]),
-        (3, top),
-        (3, bottom),
-        (3, middle),
-    )
+    d_parts = (quarters[0], quarters[3], top, bottom, middle)
+    d_table = ((0, pl.ds(0, LANES)), *((j, lanes) for j in (1, 2, 3) for lanes in d_parts))
 
     def d_copy(f, k, arriving=False):
         j, lanes = d_table[k]
@@ -150,8 +149,10 @@
 
     def pass_on(f, j):
         e_wait_recv(f, j, 1)
+        if j:
+            d_copy(f, 5 * j - 2).start()
         e_wait_recv(f, j, 0)
-        d_copy(f, j).start()
+        d_copy(f, 5 * j - 1 if j else 0).start()
 
     def near_first(f, onward):
         for part in range(2):
@@ -160,35 +161,38 @@
                 if onward:
                     x_copy(f, 6 + 3 * side + part).start()
                 e_start(f, 1 + side, part)
+                d_copy(f, 5 * side + 1 + part).start()
 
     def near_second(f, onward):
         for side in range(2):
             x_copy(f, 3 * side + 2, True).wait_recv()
             if onward:
                 x_copy(f, 8 + 3 * side).start()
+            d_copy(f, 5 * side + 5).start()
 
     def far_first(f):
         for part in range(2):
             x_copy(f, 6 + part, True).wait_recv()
             x_copy(f, 9 + part, True).wait_recv()
             e_start(f, 3, part)
-            d_copy(f, 3 + part).start()
+            d_copy(f, 11 + part).start()
 
     def far_second(f):
         x_copy(f, 8, True).wait_recv()
         x_copy(f, 11, True).wait_recv()
-        d_copy(f, 7).start()
+        d_copy(f, 15).start()
 
     def far_edges(f):
-        e_wait_recv(f, 3, 1)
-        d_copy(f, 5).start()
-        e_wait_recv(f, 3, 0)
-        d_copy(f, 6).start()
+        pass_on(f, 3)
 
     def d_wait(f, j):
         for k in range(len(d_table)):
             if d_table[k][0] == j:
                 d_copy(f, k, True).wait_recv()
+
+    def d_wait_parts(f, ks):
+        for k in ks:
+            d_copy(f, k, True).wait_recv()
 
     def products(buf, weights, pairs, start, size):
         total = None
@@ -226,7 +230,13 @@
                     buf[rows_of(chip, core), bottom] = jnp.zeros((CH, COLS), BF16)
 
     with jax.named_scope("barrier_wait"):
-        pl.semaphore_wait(barrier, TILES + CHANS - 2)
+        @pl.when(across_up | across_down)
+        def _():
+            pl.semaphore_wait(barrier, 6 + CHANS)
+
+        @pl.when(jnp.logical_not(across_up | across_down))
+        def _():
+            pl.semaphore_wait(barrier, 6 + CHANS - 1)
     with jax.named_scope("first_sends"):
         own_start(G, 0)
         own_start(G, 1)
@@ -253,16 +263,25 @@
             for k in range(4):
                 upper, lower = sent[: PACK // 2, k * 128 : (k + 1) * 128], sent[PACK // 2 :, k * 128 : (k + 1) * 128]
                 to = 2 * (part * 4 + k)
-                packed[to] = jnp.where(lane < CAP, upper, pltpu.roll(lower, CAP, 1)).astype(BF16)
-                packed[to + 1] = jnp.where(lane < CAP, pltpu.roll(upper, CAP, 1), lower).astype(BF16)
-        landed[tile] = packed[tile]
+                packed[to % 4 * 4 + to // 4] = jnp.where(lane < CAP, upper, pltpu.roll(lower, CAP, 1)).astype(BF16)
+                packed[(to + 1) % 4 * 4 + (to + 1) // 4] = jnp.where(lane < CAP, pltpu.roll(upper, CAP, 1), lower).astype(BF16)
+        passing[z] = packed[pl.ds(z * 4, 4)]
 
     def s_copy(step, arriving=False):
-        other = (tile + step) % TILES
-        place = landed.at[(tile + TILES - step) % TILES]
+        other = (z + step) % 4
+        place = passing.at[(z + 4 - step) % 4]
+        device = (y * 4 + other, chan)
         if arriving:
-            return remote(place, place, s_send.at[step], s_recv.at[step], (other, chan))
-        return remote(packed.at[other], landed.at[tile], s_send.at[step], s_recv.at[step], (other, chan))
+            return remote(place, place, s_send.at[0, step], s_recv.at[0, step], device)
+        return remote(packed.at[pl.ds(other * 4, 4)], passing.at[z], s_send.at[0, step], s_recv.at[0, step], device)
+
+    def t_copy(step, arriving=False):
+        other = (y + step) % 4
+        place = landed.at[(y + 4 - step) % 4]
+        device = (other * 4 + z, chan)
+        if arriving:
+            return remote(place, place, s_send.at[1, step], s_recv.at[1, step], device)
+        return remote(passing.at[:, other], landed.at[y], s_send.at[1, step], s_recv.at[1, step], device)
 
     def w_copy(step, arriving=False):
         other = (chan + step) % CHANS
@@ -278,7 +297,7 @@
         place = wb.at[:, pl.ds(pl.multiple_of(quarter * 16, 16), 16)]
         return remote(place, place, v_send.at[step], v_recv.at[step], (other, chan))
 
-    for step in range(1, TILES):
+    for step in range(1, 4):
         s_copy(step).start()
 
     with jax.named_scope("weight_pieces"):
@@ -299,13 +318,18 @@
         wb[chan, mine] = b2[chan, mine]
 
     with jax.named_scope("station_wait"):
-        for step in range(1, TILES):
+        for step in range(1, 4):
             s_copy(step, True).wait_recv()
+        for step in range(1, 4):
+            t_copy(step).start()
+        landed[y] = passing[:, y]
+        for step in range(1, 4):
+            t_copy(step, True).wait_recv()
     with jax.named_scope("assimilate"):
         lane = lax.broadcasted_iota(jnp.int32, (PACK // 2, 128), 1)
         slabs = []
         for k in range(TILES // 2):
-            even, odd = landed[2 * k].astype(F32), landed[2 * k + 1].astype(F32)
+            even, odd = landed[k // 2, k % 2 * 2].astype(F32), landed[k // 2, k % 2 * 2 + 1].astype(F32)
             upper = jnp.where(lane < CAP, even, pltpu.roll(odd, CAP, 1))
             lower = jnp.where(lane < CAP, pltpu.roll(even, CAP, 1), odd)
             slabs.append(jnp.concatenate([upper, lower], axis=0))
@@ -368,17 +392,19 @@
         far_edges(A)
         pass_on(G, 1)
         pass_on(G, 2)
-    with jax.named_scope("wait_A3"):
-        d_wait(A, 3)
+    spans = ((0, 3 * COLS), (13 * COLS, 3 * COLS), (3 * COLS, 10 * COLS))
+
     with jax.named_scope("conv1_pass3"):
-        for number, (start, size) in enumerate(((0, 1024), (3072, 1024), (1024, BLOCK))):
+        d_wait_parts(A, (11, 12, 13, 14))
+        for number, (start, size) in enumerate(spans):
+            if number == 2:
+                d_wait_parts(A, (15,))
             lanes = pl.ds(start, size)
             value = neighbour_sum(zbuf[:, lanes] + products(aa, w1_ref, [chips[3]], start, size))
             hidden_pre[:, lanes] = value
             hidden = value * (1.0 / (1.0 + jnp.exp(-value)))
             ha[own, pl.ds(start + COLS, size)] = hidden.astype(BF16)
-            if number:
-                own_start(H, number - 1)
+        own_start(H, 0)
 
     groups = ((0, 1, 2), (3,))
     group_lanes = (pl.ds(0, 384), pl.ds(384, 128))
@@ -486,66 +512,73 @@
         d_wait(G, 1)
         d_wait(G, 2)
         weight_terms(0)
-        one_start(0)
     with jax.named_scope("pass_on_H0"):
         pass_on(H, 0)
+    with jax.named_scope("far_G"):
+        far_first(G)
+        far_second(G)
+        own_start(H, 1)
+        one_start(0)
     with jax.named_scope("conv2_pass1"):
         d_wait(H, 0)
         conv_pass(ha, w2_ref, [chips[0]], True)
+    with jax.named_scope("far_G_edges"):
+        far_edges(G)
     with jax.named_scope("near_H1"):
         near_first(H, True)
-    with jax.named_scope("far_G"):
-        far_first(G)
-        far_second(G)
-        far_edges(G)
-    with jax.named_scope("collect_0"):
-        collect(0)
     with jax.named_scope("weight_terms_1"):
         d_wait(G, 3)
         weight_terms(1)
         one_start(1)
-    with jax.named_scope("near_H2"):
-        near_second(H, True)
-        pass_on(H, 1)
-        pass_on(H, 2)
     with jax.named_scope("turn_weights"):
         for step in range(1, 4):
             v_copy(step, True).wait_recv()
         for s in range(CHANS // 2):
             two = jnp.concatenate([wb[2 * s], wb[2 * s + 1]], axis=0).astype(F32)
             wbt[:, pl.ds(s * 128, 128)] = two.T.astype(BF16)
+    def grad_hidden(block):
+        lanes = pl.ds(block * BLOCK, BLOCK)
+        grad_act = neighbour_sum(products(ga, wbt, None, block * BLOCK, BLOCK))
+        value = hidden_pre[:, lanes]
+        s = 1.0 / (1.0 + jnp.exp(-value))
+        result = (grad_act * s * (1.0 + value * (1.0 - s))).astype(BF16)
+        gh_ref[:, block * 8 : block * 8 + 8, :] = result.reshape(CH, 8, COLS)
+
+    with jax.named_scope("grad_hidden_0"):
+        grad_hidden(0)
+    with jax.named_scope("collect_0"):
+        collect(0)
+    with jax.named_scope("near_H2"):
+        near_second(H, True)
+        pass_on(H, 1)
+        pass_on(H, 2)
+    with jax.named_scope("grad_hidden_1"):
+        grad_hidden(1)
+    with jax.named_scope("collect_1"):
+        collect(1)
     with jax.named_scope("far_H1"):
         far_first(H)
-    with jax.named_scope("collect_1"):
-        collect(1)
-    with jax.named_scope("grad_hidden"):
-        for block in range(2):
-            lanes = pl.ds(block * BLOCK, BLOCK)
-            grad_act = neighbour_sum(products(ga, wbt, None, block * BLOCK, BLOCK))
-            value = hidden_pre[:, lanes]
-            s = 1.0 / (1.0 + jnp.exp(-value))
-            result = (grad_act * s * (1.0 + value * (1.0 - s))).astype(BF16)
-            gh_ref[:, block * 8 : block * 8 + 8, :] = result.reshape(CH, 8, COLS)
     with jax.named_scope("conv2_pass2"):
         d_wait(H, 1)
         d_wait(H, 2)
         conv_pass(ha, w2_ref, [chips[1], chips[2]], False)
+    with jax.named_scope("far_H2"):
+        far_second(H)
+    with jax.named_scope("far_H_edges"):
+        far_edges(H)
     with jax.named_scope("finish_0"):
         finish(0)
     with jax.named_scope("finish_1"):
         finish(1)
-    with jax.named_scope("far_H2"):
-        far_second(H)
-    with jax.named_scope("far_H_edges"):
-        far_edges(H)
-    with jax.named_scope("wait_H3"):
-        d_wait(H, 3)
     with jax.named_scope("conv2_pass3"):
-        for block in range(2):
-            lanes = pl.ds(block * BLOCK, BLOCK)
-            branch = neighbour_sum(zbuf[:, lanes] + products(ha, w2_ref, [chips[3]], block * BLOCK, BLOCK))
-            result = (aa[own, pl.ds(block * BLOCK + COLS, BLOCK)].astype(F32) + branch).astype(BF16)
-            out_ref[:, block * 8 : block * 8 + 8, :] = result.reshape(CH, 8, COLS)
+        d_wait_parts(H, (11, 12, 13, 14))
+        for number, (start, size) in enumerate(spans):
+            if number == 2:
+                d_wait_parts(H, (15,))
+            lanes = pl.ds(start, size)
+            branch = neighbour_sum(zbuf[:, lanes] + products(ha, w2_ref, [chips[3]], start, size))
+            hidden_pre[:, lanes] = aa[own, pl.ds(start + COLS, size)].astype(F32) + branch
+        out_ref[...] = hidden_pre[...].astype(BF16).reshape(CH, ROWS, COLS)
     with jax.named_scope("grad_weight"):
         @pl.when(jnp.logical_not(owns))
         def _():
@@ -572,8 +605,9 @@
                 def _(f=f, j=j):
                     e_copy(f, j, 1).wait_send()
 
-        for step in range(1, TILES):
+        for step in range(1, 4):
             s_copy(step).wait_send()
+            t_copy(step).wait_send()
         for step in range(1, CHANS):
             w_copy(step).wait_send()
         for step in range(1, 4):
@@ -648,7 +682,8 @@
             pltpu.VMEM((CHANS, CH, 10 * CH), BF16),
             pltpu.VMEM((10 * CH, ALL), BF16),
             pltpu.VMEM((TILES, PACK // 2, 128), BF16),
-            pltpu.VMEM((TILES, PACK // 2, 128), BF16),
+            pltpu.VMEM((4, 4, PACK // 2, 128), BF16),
+            pltpu.VMEM((4, 4, PACK // 2, 128), BF16),
             pltpu.VMEM((ROWS * CH, TILES * CAP), BF16),
             pltpu.VMEM((2, 3, 96, ALL), BF16),
             pltpu.VMEM((3, 3, 96, ALL), BF16),
@@ -656,8 +691,8 @@
             pltpu.VMEM((3, 3, 96, ALL), BF16),
             pltpu.VMEM((4, 2, 144, 128), BF16),
             pltpu.VMEM((144, 128), BF16),
-            dma((3, 12)), dma((3, 12)), dma((3, 8)), dma((3, 8)), dma((3, 8)), dma((3, 8)),
-            dma((TILES,)), dma((TILES,)), dma((CHANS,)), dma((CHANS,)), dma((4,)), dma((4,)),
+            dma((3, 12)), dma((3, 12)), dma((3, 8)), dma((3, 8)), dma((3, 16)), dma((3, 16)),
+            dma((2, 4)), dma((2, 4)), dma((CHANS,)), dma((CHANS,)), dma((4,)), dma((4,)),
             dma((2, 2)), dma((3, 2)), dma((2,)), dma((3, 2)), dma((4, 2)), dma((1,)),
         ],
         compiler_params=pltpu.CompilerParams(

time: 81.5 us -> 77.2 us (0.947); the launches traced: 80.2 us -> 77 us
  Pallas kernels: 79.4 us -> 76.2 us
    pallas_call x1, Pallas kernels: 77.2 us -> 74 us  [local(): pl.pallas_call(kernel, out_shape=(jax.ShapeDtypeStruct((CH, ROWS, COLS),...]
where the time goes in v2:
time: 77.2 us; the launch traced here: 77 us
  Pallas kernels  76.2 us (99%)
  between operations  0.8 us (1%)
    pallas_call x1, Pallas kernels, local(): pl.pallas_call(kernel, out_shape=(jax.ShapeDtypeStruct((CH, ROWS, COLS),...  74 us
    pallas_call x1, Pallas kernels, local(): pl.pallas_call(hand_over, out_shape=tuple((jax.ShapeDtypeStruct(result.sh...  2.14 us

profile of v2, /device:TPU:5, one launch (start us, length us, event | category | flops | bytes accessed | tf_op | source)
XLA Modules:
  0.0 77.0 jit_solution(1787909710888989403)
XLA Ops:
  0.6 74.0 %shard_map.103 = (bf16[64,16,256]{2,1,0:T(8,128)(2,1)}, bf16[3,3,32,64]{3,2,1,0:T(8,128)(2,1)}, bf16[64,16,256]{2,1,0:T(8,128)(2,1)}) custom-call(bf16[64,512]{1,0:T(8,128)(2,1)} %feats_ref.1, s32[1,512]{1,0:T(1,128)} %bitcast.11, s32[1,512]{1,0:T(1,128)} %bitcast.12, s32[1,512]{1,0:T(1,128)} %bitcast.13, bf16[64,16,256]{2,1,0:T(8,128)(2,1)} %gout_hbm.1, ...), custom_call_target="tpu_custom_call" | custom-call | tf_op jit(solution)/shard_map/pallas_call | solution.py:660
  74.7 2.1 %shard_map.104 = (bf16[64,16,256]{2,1,0:T(8,128)(2,1)}, bf16[3,3,32,64]{3,2,1,0:T(8,128)(2,1)}, bf16[64,16,256]{2,1,0:T(8,128)(2,1)}) custom-call(bf16[64,16,256]{2,1,0:T(8,128)(2,1)} %get-tuple-element.6.out_from, bf16[3,3,32,64]{3,2,1,0:T(8,128)(2,1)} %get-tuple-element.7.gw_from, bf16[64,16,256]{2,1,0:T(8,128)(2,1)} %get-tuple-element.8.gh_from), custom_call_target="tpu_custom_call" | custom-call | tf_op jit(solution)/shard_map/pallas_call | solution.py:711

commit v3 on v2

--- a/solution.py
+++ b/solution.py
@@ -44,7 +44,7 @@
     out_ref, gw_ref, gh_ref,
     gout_ref, grid_ref, w1_ref, w2_ref, in_sem, ga, aa, ha, zbuf, hidden_pre, h3, b2, wb, wbt, packed, passing, landed, masked,
     gw_out, gw_one, gw_mid, gw_two, gw_fin, gw_land,
-    x_send, x_recv, e_send, e_recv, d_send, d_recv, s_send, s_recv, w_send, w_recv, v_send, v_recv,
+    x_send, x_recv, e_send, e_recv, d_send, d_recv, s_send, s_recv, w_send, w_recv, u_send, u_recv, v_send, v_recv,
     one_send, one_recv, two_send, two_recv, three_send, three_recv,
 ):
     tile = lax.axis_index("tile")
@@ -283,13 +283,26 @@
             return remote(place, place, s_send.at[1, step], s_recv.at[1, step], device)
         return remote(passing.at[:, other], landed.at[y], s_send.at[1, step], s_recv.at[1, step], device)
 
-    def w_copy(step, arriving=False):
+    z_rows = pl.ds(pl.multiple_of(z * 16, 16), 16)
+    y_halves = (pl.ds(0, 384), pl.ds(384, 256))
+
+    def by_half(act, turned=False):
+        for half in range(2):
+            @pl.when((y + turned) % 2 == half)
+            def _(half=half):
+                act(half)
+
+    def w_copy(step, half, arriving=False):
         other = (chan + step) % CHANS
-        rows = pl.ds(pl.multiple_of(z * 16, 16), 16)
-        place = wb.at[(chan + CHANS - step) % CHANS, rows]
+        lanes = y_halves[half]
+        place = wb.at[(chan + CHANS - step) % CHANS, z_rows, lanes]
         if arriving:
             return remote(place, place, w_send.at[step], w_recv.at[step], (tile, other))
-        return remote(b2.at[other, rows], wb.at[chan, rows], w_send.at[step], w_recv.at[step], (tile, other))
+        return remote(b2.at[other, z_rows, lanes], wb.at[chan, z_rows, lanes], w_send.at[step], w_recv.at[step], (tile, other))
+
+    def u_copy(half):
+        place = wb.at[:, z_rows, y_halves[half]]
+        return remote(place, place, u_send.at[0], u_recv.at[0], ((y + 1 - 2 * (y % 2)) * 4 + z, chan))
 
     def v_copy(step, arriving=False):
         other = y * 4 + (z + step) % 4
@@ -312,10 +325,12 @@
                 odd = jnp.where(lane < CH, turned[n], taps[n + 1] if n < 8 else 0.0)
                 b2[2 * chip, :, pl.ds(k * 128, 128)] = even.astype(BF16)
                 b2[2 * chip + 1, :, pl.ds(k * 128, 128)] = odd.astype(BF16)
-        for step in range(1, CHANS):
-            w_copy(step).start()
-        mine = pl.ds(pl.multiple_of(z * 16, 16), 16)
-        wb[chan, mine] = b2[chan, mine]
+        def weights_out(half):
+            for step in range(1, CHANS):
+                w_copy(step, half).start()
+            wb[chan, z_rows, y_halves[half]] = b2[chan, z_rows, y_halves[half]]
+
+        by_half(weights_out)
 
     with jax.named_scope("station_wait"):
         for step in range(1, 4):
@@ -362,16 +377,21 @@
         inward[3].wait()
         conv_pass(aa, w1_ref, [chips[0]], True)
     with jax.named_scope("weights_round"):
-        for step in range(1, CHANS):
-            w_copy(step, True).wait_recv()
-        for step in range(1, 4):
-            v_copy(step).start()
+        def weights_on(half):
+            for step in range(1, CHANS):
+                w_copy(step, half, True).wait_recv()
+            u_copy(half).start()
+
+        by_half(weights_on)
     with jax.named_scope("near_G1"):
         near_first(G, False)
     with jax.named_scope("near_A1"):
         near_first(A, True)
     with jax.named_scope("near_G2"):
         near_second(G, False)
+        by_half(lambda half: u_copy(half).wait_recv(), True)
+        for step in range(1, 4):
+            v_copy(step).start()
     with jax.named_scope("near_A2"):
         near_second(A, True)
     with jax.named_scope("pass_on_A12"):
@@ -608,8 +628,12 @@
         for step in range(1, 4):
             s_copy(step).wait_send()
             t_copy(step).wait_send()
-        for step in range(1, CHANS):
-            w_copy(step).wait_send()
+        def weights_left(half):
+            for step in range(1, CHANS):
+                w_copy(step, half).wait_send()
+            u_copy(half).wait_send()
+
+        by_half(weights_left)
         for step in range(1, 4):
             v_copy(step).wait_send()
         for group in range(2):
@@ -692,7 +716,7 @@
             pltpu.VMEM((4, 2, 144, 128), BF16),
             pltpu.VMEM((144, 128), BF16),
             dma((3, 12)), dma((3, 12)), dma((3, 8)), dma((3, 8)), dma((3, 16)), dma((3, 16)),
-            dma((2, 4)), dma((2, 4)), dma((CHANS,)), dma((CHANS,)), dma((4,)), dma((4,)),
+            dma((2, 4)), dma((2, 4)), dma((CHANS,)), dma((CHANS,)), dma((1,)), dma((1,)), dma((4,)), dma((4,)),
             dma((2, 2)), dma((3, 2)), dma((2,)), dma((3, 2)), dma((4, 2)), dma((1,)),
         ],
         compiler_params=pltpu.CompilerParams(

time: 77.2 us -> 76.1 us (0.986)
  Pallas kernels: 76.2 us -> 75.1 us
    pallas_call x1, Pallas kernels: 74 us -> 73 us  [local(): pl.pallas_call(kernel, out_shape=(jax.ShapeDtypeStruct((CH, ROWS, COLS),...]
where the time goes in v3:
time: 76.1 us; the launch traced here: 75.9 us
  Pallas kernels  75.1 us (99%)
  between operations  0.8 us (1%)
    pallas_call x1, Pallas kernels, local(): pl.pallas_call(kernel, out_shape=(jax.ShapeDtypeStruct((CH, ROWS, COLS),...  73 us
    pallas_call x1, Pallas kernels, local(): pl.pallas_call(hand_over, out_shape=tuple((jax.ShapeDtypeStruct(result.sh...  2.14 us

profile of v3, /device:TPU:5, one launch (start us, length us, event | category | flops | bytes accessed | tf_op | source)
XLA Modules:
  0.0 75.9 jit_solution(18048855992993956684)
XLA Ops:
  0.6 73.0 %shard_map.103 = (bf16[64,16,256]{2,1,0:T(8,128)(2,1)}, bf16[3,3,32,64]{3,2,1,0:T(8,128)(2,1)}, bf16[64,16,256]{2,1,0:T(8,128)(2,1)}) custom-call(bf16[64,512]{1,0:T(8,128)(2,1)} %feats_ref.1, s32[1,512]{1,0:T(1,128)} %bitcast.11, s32[1,512]{1,0:T(1,128)} %bitcast.12, s32[1,512]{1,0:T(1,128)} %bitcast.13, bf16[64,16,256]{2,1,0:T(8,128)(2,1)} %gout_hbm.1, ...), custom_call_target="tpu_custom_call" | custom-call | tf_op jit(solution)/shard_map/pallas_call | solution.py:684
  73.6 2.1 %shard_map.104 = (bf16[64,16,256]{2,1,0:T(8,128)(2,1)}, bf16[3,3,32,64]{3,2,1,0:T(8,128)(2,1)}, bf16[64,16,256]{2,1,0:T(8,128)(2,1)}) custom-call(bf16[64,16,256]{2,1,0:T(8,128)(2,1)} %get-tuple-element.6.out_from, bf16[3,3,32,64]{3,2,1,0:T(8,128)(2,1)} %get-tuple-element.7.gw_from, bf16[64,16,256]{2,1,0:T(8,128)(2,1)} %get-tuple-element.8.gh_from), custom_call_target="tpu_custom_call" | custom-call | tf_op jit(solution)/shard_map/pallas_call | solution.py:735

commit v4 on v3

--- a/solution.py
+++ b/solution.py
@@ -41,7 +41,8 @@
 
 def kernel(
     feats_ref, owner_ref, valid_ref, cell_ref, gout_hbm, grid_hbm, w1_hbm, w2_hbm,
-    out_ref, gw_ref, gh_ref,
+    out_hbm, gw_hbm, gh_hbm,
+    out_ref, gw_ref, gh_ref, out_sem,
     gout_ref, grid_ref, w1_ref, w2_ref, in_sem, ga, aa, ha, zbuf, hidden_pre, h3, b2, wb, wbt, packed, passing, landed, masked,
     gw_out, gw_one, gw_mid, gw_two, gw_fin, gw_land,
     x_send, x_recv, e_send, e_recv, d_send, d_recv, s_send, s_recv, w_send, w_recv, u_send, u_recv, v_send, v_recv,
@@ -66,6 +67,10 @@
     ]
     for copy in inward:
         copy.start()
+    outward = [
+        pltpu.make_async_copy(src, dst, out_sem.at[k])
+        for k, (src, dst) in enumerate(((gh_ref, gh_hbm), (out_ref, out_hbm), (gw_ref, gw_hbm)))
+    ]
 
     barrier = pltpu.get_barrier_semaphore()
     across_up, across_down = has_up & (z == 0), has_down & (z == 3)
@@ -574,6 +579,7 @@
         pass_on(H, 2)
     with jax.named_scope("grad_hidden_1"):
         grad_hidden(1)
+        outward[0].start()
     with jax.named_scope("collect_1"):
         collect(1)
     with jax.named_scope("far_H1"):
@@ -599,6 +605,7 @@
             branch = neighbour_sum(zbuf[:, lanes] + products(ha, w2_ref, [chips[3]], start, size))
             hidden_pre[:, lanes] = aa[own, pl.ds(start + COLS, size)].astype(F32) + branch
         out_ref[...] = hidden_pre[...].astype(BF16).reshape(CH, ROWS, COLS)
+        outward[1].start()
     with jax.named_scope("grad_weight"):
         @pl.when(jnp.logical_not(owns))
         def _():
@@ -609,6 +616,8 @@
         for n in range(18):
             rows = sides[n // 9][(n % 9) * 16 : (n % 9) * 16 + 16]
             gw_ref[n // 6, n % 6 // 2, pl.ds(n % 2 * 16, 16), :] = rows
+
+        outward[2].start()
 
     with jax.named_scope("sends_done"):
         for f in (G, A, H):
@@ -656,6 +665,8 @@
                             three_copy(j, which).wait_send()
                     else:
                         three_copy(j, which).wait_send()
+        for copy in outward:
+            copy.wait()
 
 
 def hand_over(out_from, gw_from, gh_from, out_to, gw_to, gh_to, out_via, gw_via, gh_via, sems):
@@ -689,8 +700,12 @@
             jax.ShapeDtypeStruct((CH, ROWS, COLS), BF16),
         ),
         in_specs=[vmem] * 4 + [whole] * 4,
-        out_specs=(vmem,) * 3,
+        out_specs=(whole,) * 3,
         scratch_shapes=[
+            pltpu.VMEM((CH, ROWS, COLS), BF16),
+            pltpu.VMEM((3, 3, PART, CH), BF16),
+            pltpu.VMEM((CH, ROWS, COLS), BF16),
+            dma((3,)),
             pltpu.VMEM((CH, ROWS, COLS), BF16),
             pltpu.VMEM((CH, ROWS, COLS), BF16),
             pltpu.VMEM((9 * CH, ALL), BF16),

time: 76.1 us -> 75.6 us (level)
  no operation moved by 1% of the time
where the time goes in v4:
time: 75.6 us; the launch traced here: 75.4 us
  Pallas kernels  74.6 us (99%)
  between operations  0.8 us (1%)
    pallas_call x1, Pallas kernels, local(): pl.pallas_call(kernel, out_shape=(jax.ShapeDtypeStruct((CH, ROWS, COLS),...  72.5 us
    pallas_call x1, Pallas kernels, local(): pl.pallas_call(hand_over, out_shape=tuple((jax.ShapeDtypeStruct(result.sh...  2.14 us

profile of v4, /device:TPU:5, one launch (start us, length us, event | category | flops | bytes accessed | tf_op | source)
XLA Modules:
  0.0 75.4 jit_solution(939811726181580356)
XLA Ops:
  0.6 72.5 %shard_map.103 = (bf16[64,16,256]{2,1,0:T(8,128)(2,1)}, bf16[3,3,32,64]{3,2,1,0:T(8,128)(2,1)}, bf16[64,16,256]{2,1,0:T(8,128)(2,1)}) custom-call(bf16[64,512]{1,0:T(8,128)(2,1)} %feats_ref.1, s32[1,512]{1,0:T(1,128)} %bitcast.11, s32[1,512]{1,0:T(1,128)} %bitcast.12, s32[1,512]{1,0:T(1,128)} %bitcast.13, bf16[64,16,256]{2,1,0:T(8,128)(2,1)} %gout_hbm.1, ...), custom_call_target="tpu_custom_call" | custom-call | tf_op jit(solution)/shard_map/pallas_call | solution.py:695
  73.1 2.1 %shard_map.104 = (bf16[64,16,256]{2,1,0:T(8,128)(2,1)}, bf16[3,3,32,64]{3,2,1,0:T(8,128)(2,1)}, bf16[64,16,256]{2,1,0:T(8,128)(2,1)}) custom-call(bf16[64,16,256]{2,1,0:T(8,128)(2,1)} %get-tuple-element.6.out_from, bf16[3,3,32,64]{3,2,1,0:T(8,128)(2,1)} %get-tuple-element.7.gw_from, bf16[64,16,256]{2,1,0:T(8,128)(2,1)} %get-tuple-element.8.gh_from), custom_call_target="tpu_custom_call" | custom-call | tf_op jit(solution)/shard_map/pallas_call | solution.py:750
